TPU v7x, 32 devices: a whole 2x2x4 slice. The times are simulated.
32 devices in a mesh: horiz: 8 (over z, x), depth: 4 (over y, core).
Axes of the slice: x: 2, y: 2, z: 4, core: 2. Of those that a mesh axis runs over, the one named last changes fastest.
Arguments:
- adjoint_seed: bfloat16 [16, 48, 8192], P(None, 'depth', 'horiz'), may hold values from -6 to 6
- transport: bfloat16 [48, 64, 5, 128, 128], P('depth', 'horiz'), may hold values from -0.25 to 0.25
- neighbours: int32 [64, 5], P('horiz'), may hold values from 0 to 63, as said below
- inv_mix: float32 [48, 48, 8192], P(None, None, ('horiz', 'depth')), may hold values from -0.875 to 0.875
- rates: float32 [48, 8192], P('depth', 'horiz'), may hold values from 0.2 to 2
- coupling: float32 [16, 16], replicated, may hold values from -1.5 to 1.5
- sensitivity: bfloat16 [16, 48, 8192], P(None, 'depth', 'horiz')
- depth_count: int32 [8192], P('horiz'), may hold values from 0 to 48, as said below
Outputs:
- first: bfloat16 [16, 48, 8192], P(None, 'depth', 'horiz')
- second: bfloat16 [16, 48, 8192], P(None, 'depth', 'horiz')
- gradient: float32 [16], replicated
Inputs may be any that keep to these rules, and one draw needn't show every extreme that they name: neighbours[b, 0] = b; every entry lies within 8 blocks of its row's block b, counted cyclically over 64 blocks. `depth_count`: 0 marks a land column.
All inputs are finite; a program needn't handle non-finite values.
Results may differ from a plain program's by a relative error of at most 0.011.
Values may be sent and summed in bfloat16 or wider, within the bound.
A program may use at most 128 MiB of HBM per device.

v0:
```python
import math

import jax
import jax.numpy as jnp
from jax import lax
from jax.sharding import PartitionSpec as P


def padded(cells, sides, width):
    for axis, dim in sides:
        count = lax.axis_size(axis)
        head = lax.slice_in_dim(cells, 0, width, axis=dim)
        tail = lax.slice_in_dim(cells, cells.shape[dim] - width, cells.shape[dim], axis=dim)
        cells = jnp.concatenate(
            [
                lax.ppermute(tail, axis, [(i, (i + 1) % count) for i in range(count)]),
                cells,
                lax.ppermute(head, axis, [((i + 1) % count, i) for i in range(count)]),
            ],
            axis=dim,
        )
    return cells


def per_device(
    adjoint_seed, transport, neighbours, inv_mix, rates, coupling, sensitivity, depth_count
):
    tracers, lev_dev, cols = adjoint_seed.shape
    blocks, slots = neighbours.shape
    width = transport.shape[3]
    total_blocks = blocks * lax.axis_size("horiz")
    levels = lev_dev * lax.axis_size("depth")
    row_ids = lax.axis_index("horiz") * blocks + jnp.arange(blocks, dtype=jnp.int32)
    offset = (neighbours - row_ids[:, None] + blocks) % total_blocks - blocks
    source_rows = (jnp.arange(blocks, dtype=jnp.int32)[:, None] + blocks + offset).reshape(-1)
    level_ids = (
        lax.broadcasted_iota(jnp.int32, (lev_dev, cols), 0) + lax.axis_index("depth") * lev_dev
    )
    wet = (level_ids < depth_count[None, :]).astype(jnp.float32)
    sens = sensitivity.astype(jnp.float32)
    state = adjoint_seed
    results = []
    partials = []
    for step in range(2):
        full = lax.all_to_all(state, "depth", split_axis=2, concat_axis=1, tiled=True)
        mixed_cols = jnp.einsum(
            "pqc,tpc->tqc", inv_mix, full.astype(jnp.float32), precision=lax.Precision.HIGHEST
        ).astype(jnp.bfloat16)
        mixed = lax.all_to_all(mixed_cols, "depth", split_axis=1, concat_axis=2, tiled=True)
        mixed_f = mixed.astype(jnp.float32)
        grouped = mixed.reshape(tracers, lev_dev, blocks, width)
        nearby = padded(grouped, (("horiz", 2),), blocks)
        picked = jnp.take(nearby, source_rows, axis=2).reshape(
            tracers, lev_dev, blocks, slots, width
        )
        moved = jnp.einsum(
            "lrkij,tlrkj->tlri", transport, picked, preferred_element_type=jnp.float32
        )
        moved = moved.reshape(tracers, lev_dev, cols)
        source_term = rates[None, :, :] * jnp.einsum(
            "ut,ulc->tlc", coupling, mixed_f, precision=lax.Precision.HIGHEST
        )
        new_state = (wet[None] * (moved + source_term - state.astype(jnp.float32))).astype(
            jnp.bfloat16
        )
        local_terms = jnp.sum(wet[None] * mixed_f * sens, axis=(1, 2))
        partials.append(lax.psum(local_terms, ("horiz", "depth")))
        results.append(new_state)
        state = new_state
    grad_total = partials[0] + partials[1]
    gradient = grad_total / math.sqrt(levels * total_blocks * width)
    return (results[0], results[1], gradient)


def solution(mesh):
    return jax.shard_map(
        per_device,
        mesh=mesh,
        in_specs=(
            P(None, "depth", "horiz"),
            P("depth", "horiz", None, None, None),
            P("horiz", None),
            P(None, None, ("horiz", "depth")),
            P("depth", "horiz"),
            P(),
            P(None, "depth", "horiz"),
            P("horiz"),
        ),
        out_specs=(P(None, "depth", "horiz"), P(None, "depth", "horiz"), P()),
        check_vma=False,
    )
```

profile of v0, /device:TPU:0, one launch (start us, length us, event | category | flops | bytes accessed | tf_op | source)
XLA Modules:
  0.0 201.4 jit_solution(4085397204308225338)
XLA Ops:
  0.6 5.7 %copy.89 = bf16[16,12,1024]{0,1,2:T(8,128)(2,1)} copy(bf16[16,12,1024]{2,0,1:T(8,128)(2,1)} %param.10) | data formatting | bytes 786432 | tf_op args[0]
  6.3 5.9 %reshape.103 = bf16[4,2,24576]{2,1,0:T(2,128)(2,1)} reshape(bf16[1024,12,16]{2,1,0:T(8,128)(2,1)} %bitcast.82) | data formatting | bytes 786432
  12.2 4.2 %all-to-all-start = ((bf16[4,2,24576]{2,1,0:T(2,128)(2,1)}), bf16[4,2,24576]{2,1,0:T(2,128)(2,1)S(1)}, u32[]{:S(2)}, u32[]{:S(2)}) async-start(bf16[4,2,24576]{2,1,0:T(2,128)(2,1)} %reshape.103), calls=%async_computation | async-start | bytes 786432 | tf_op jit(solution)/shard_map/all_to_all | solution.py:45
  16.5 0.1 fusion.28
  16.5 0.1 reshape.71
  16.6 5.2 %copy.93 = f32[48,48,256]{1,0,2:T(8,128)} copy(f32[48,48,256]{2,1,0:T(8,128)S(1)} %copy-done.5) | data formatting | bytes 4718592 | tf_op args[3]
  21.9 2.0 %all-to-all-done = bf16[4,2,24576]{2,1,0:T(2,128)(2,1)S(1)} async-done(((bf16[4,2,24576]{2,1,0:T(2,128)(2,1)}), bf16[4,2,24576]{2,1,0:T(2,128)(2,1)S(1)}, u32[]{:S(2)}, u32[]{:S(2)}) %all-to-all-start) | async-done | bytes 393248 | tf_op jit(solution)/shard_map/all_to_all | solution.py:45
  23.9 4.9 %reshape.104 = bf16[1024,12,16]{2,1,0:T(8,128)(2,1)} reshape(bf16[4,2,24576]{2,1,0:T(2,128)(2,1)S(1)} %all-to-all-done) | data formatting | bytes 786432
  28.8 4.9 %copy.121 = bf16[16,12,4,256]{3,2,0,1:T(4,128)(2,1)S(1)} copy(bf16[16,12,4,256]{0,1,3,2:T(8,128)(2,1)} %bitcast.80) | data formatting | bytes 786432 | tf_op jit(solution)/shard_map/all_to_all | solution.py:45
  33.8 1.2 copy.92
  35.0 5.1 %fusion.4 = bf16[16,48,256]{1,0,2:T(8,128)(2,1)S(1)} fusion(bf16[16,48,256]{1,0,2:T(8,128)(2,1)S(1)} %copy.92, f32[48,48,256]{1,0,2:T(8,128)} %copy.93), kind=kOutput, calls=%fused_computation.10 | convolution fusion | flops 113442816 | bytes 3145728 | tf_op jit(solution)/shard_map/pqc,tpc->tqc/dot_general | solution.py:46
  40.1 2.0 copy.94
  42.0 3.5 %all-to-all-start.1 = ((bf16[16,48,256]{2,0,1:T(8,128)(2,1)}), bf16[16,48,256]{2,0,1:T(8,128)(2,1)S(1)}, u32[]{:S(2)}, u32[]{:S(2)}) async-start(bf16[16,48,256]{2,0,1:T(8,128)(2,1)} %copy.94), calls=%async_computation.1 | async-start | bytes 786432 | tf_op jit(solution)/shard_map/all_to_all | solution.py:49
  45.5 7.4 %all-to-all-done.1 = bf16[16,48,256]{2,0,1:T(8,128)(2,1)S(1)} async-done(((bf16[16,48,256]{2,0,1:T(8,128)(2,1)}), bf16[16,48,256]{2,0,1:T(8,128)(2,1)S(1)}, u32[]{:S(2)}, u32[]{:S(2)}) %all-to-all-start.1) | async-done | bytes 393248 | tf_op jit(solution)/shard_map/all_to_all | solution.py:49
  52.9 0.3 copy.95
  53.2 0.2 reshape.70
  53.4 0.2 copy.96
  53.6 5.2 %collective-permute-start.1 = (bf16[16,12,8,128]{3,0,2,1:T(8,128)(2,1)S(1)}, bf16[16,12,8,128]{3,0,2,1:T(8,128)(2,1)S(1)}, u32[]{:S(2)}, u32[]{:S(2)}) collective-permute-start(bf16[16,12,8,128]{3,0,2,1:T(8,128)(2,1)S(1)} %copy.96), channel_id=1, source_target_pairs={{4,0},{8,4},{12,8},{16,12},{20,16},{24,20},{28,24},{0,28},{5,1},{9... | collective-permute-start | bytes 1179656 | tf_op jit(solution)/shard_map/ppermute | solution.py:18
  58.8 0.7 compare_convert_fusion
  59.5 0.8 copy.126
  60.3 12.8 %collective-permute-done.1 = bf16[16,12,8,128]{3,0,2,1:T(8,128)(2,1)S(1)} collective-permute-done((bf16[16,12,8,128]{3,0,2,1:T(8,128)(2,1)S(1)}, bf16[16,12,8,128]{3,0,2,1:T(8,128)(2,1)S(1)}, u32[]{:S(2)}, u32[]{:S(2)}) %collective-permute-start.1) | collective-permute-done | bytes 393248 | tf_op jit(solution)/shard_map/ppermute | solution.py:18
  73.1 0.2 collective-permute-done
  73.2 0.1 pad_maximum_fusion
  73.4 1.0 gather_fusion
  74.4 1.6 broadcast_select_fusion.1
  76.0 8.7 %fusion.6 = f32[12,8,2,8,128]{4,3,2,1,0:T(8,128)S(1)} fusion(bf16[12,8,5,128,128]{4,3,2,1,0:T(8,128)(2,1)} %param.11, bf16[16,12,8,5,128]{4,0,1,3,2:T(8,128)(2,1)} %bitcast.85), kind=kOutput, calls=%fused_computation.12 | convolution fusion | flops 251658240 | bytes 18481152 | tf_op jit(solution)/shard_map/lrkij,tlrkj->tlri/dot_general | solution.py:56
  84.8 0.7 fusion.20
  85.5 4.7 %copy.103 = bf16[16,12,1024]{0,1,2:T(8,128)(2,1)} copy(bf16[16,12,1024]{2,0,1:T(8,128)(2,1)S(1)} %fusion.20) | data formatting | bytes 786432 | tf_op jit(solution)/shard_map/convert_element_type | solution.py:63
  90.2 5.1 %reshape.105 = bf16[4,2,24576]{2,1,0:T(2,128)(2,1)S(1)} reshape(bf16[1024,12,16]{2,1,0:T(8,128)(2,1)} %bitcast.83) | data formatting | bytes 786432
  95.3 9.8 %all_to_all.72 = bf16[4,2,24576]{2,1,0:T(2,128)(2,1)S(1)} all-to-all(bf16[4,2,24576]{2,1,0:T(2,128)(2,1)S(1)} %reshape.105), channel_id=1, replica_groups=mesh['horiz'=8,'depth'=4] {'depth'}, dimensions={0} | all-to-all | bytes 786432 | tf_op jit(solution)/shard_map/all_to_all | solution.py:45
  105.1 4.9 %reshape.106 = bf16[1024,12,16]{2,1,0:T(8,128)(2,1)} reshape(bf16[4,2,24576]{2,1,0:T(2,128)(2,1)S(1)} %all_to_all.72) | data formatting | bytes 786432
  110.0 4.9 %copy.123 = bf16[16,12,4,256]{3,2,0,1:T(4,128)(2,1)S(1)} copy(bf16[16,12,4,256]{0,1,3,2:T(8,128)(2,1)} %bitcast.81) | data formatting | bytes 786432 | tf_op jit(solution)/shard_map/all_to_all | solution.py:45
  115.0 1.2 copy.106
  116.2 5.1 %fusion.5 = bf16[16,48,256]{1,0,2:T(8,128)(2,1)S(1)} fusion(bf16[16,48,256]{1,0,2:T(8,128)(2,1)S(1)} %copy.106, f32[48,48,256]{1,0,2:T(8,128)} %copy.93), kind=kOutput, calls=%fused_computation.11 | convolution fusion | flops 113442816 | bytes 3145728 | tf_op jit(solution)/shard_map/pqc,tpc->tqc/dot_general | solution.py:46
  121.3 1.2 copy.108
  122.5 10.0 %all_to_all.73 = bf16[16,48,256]{2,0,1:T(8,128)(2,1)S(1)} all-to-all(bf16[16,48,256]{2,0,1:T(8,128)(2,1)S(1)} %copy.108), channel_id=1, replica_groups=mesh['horiz'=8,'depth'=4] {'depth'}, dimensions={1} | all-to-all | bytes 786432 | tf_op jit(solution)/shard_map/all_to_all | solution.py:49
  132.5 0.3 copy.109
  132.8 0.2 reshape.74
  132.9 0.2 copy.110
  133.1 4.9 %collective-permute-start.3 = (bf16[16,12,8,128]{3,0,2,1:T(8,128)(2,1)S(1)}, bf16[16,12,8,128]{3,0,2,1:T(8,128)(2,1)S(1)}, u32[]{:S(2)}, u32[]{:S(2)}) collective-permute-start(bf16[16,12,8,128]{3,0,2,1:T(8,128)(2,1)S(1)} %copy.110), channel_id=1, source_target_pairs={{4,0},{8,4},{12,8},{16,12},{20,16},{24,20},{28,24},{0,28},{5,1},{9... | collective-permute-start | bytes 1179656 | tf_op jit(solution)/shard_map/ppermute | solution.py:18
  138.1 0.4 fusion.23
  138.5 48.5 %psum.16 = f32[16]{0:T(128)S(1)} all-reduce(f32[16]{0:T(128)S(1)} %add.73), channel_id=1, replica_groups=mesh['horiz'=8,'depth'=4] {'horiz','depth'}, use_global_device_ids=true, to_apply=%region_1.3 | all-reduce | flops 16 | bytes 128 | tf_op jit(solution)/shard_map/psum | solution.py:67
  187.0 0.5 broadcast_multiply_fusion
  187.5 1.1 pad_maximum_fusion.1
  188.7 1.0 gather_fusion.1
  189.7 1.6 broadcast_select_fusion
  191.3 8.7 %fusion.9 = f32[12,8,2,8,128]{4,3,2,1,0:T(8,128)S(1)} fusion(bf16[12,8,5,128,128]{4,3,2,1,0:T(8,128)(2,1)} %param.11, bf16[16,12,8,5,128]{4,0,1,3,2:T(8,128)(2,1)} %bitcast.84), kind=kOutput, calls=%fused_computation.13 | convolution fusion | flops 251658240 | bytes 18481152 | tf_op jit(solution)/shard_map/lrkij,tlrkj->tlri/dot_general | solution.py:56
  200.0 1.4 fusion.21
  (41 shorter events, 0.3 us)
Async XLA Ops:
  0.6 84.1 %copy-start = (f32[16,16]{1,0:T(8,128)S(1)}, f32[16,16]{1,0:T(8,128)}, u32[]{:S(2)}) copy-start(f32[16,16]{1,0:T(8,128)} %param.15) | copy-start | bytes 3076
  6.3 10.1 %copy-start.13 = (s32[8,5]{1,0:T(8,128)S(1)}, s32[8,5]{1,0:T(8,128)}, u32[]{:S(2)}) copy-start(s32[8,5]{1,0:T(8,128)} %param.12) | copy-start | bytes 484
  6.3 10.3 %copy-start.5 = (f32[48,48,256]{2,1,0:T(8,128)S(1)}, f32[48,48,256]{2,1,0:T(8,128)}, u32[]{:S(2)}) copy-start(f32[48,48,256]{2,1,0:T(8,128)} %param.13) | copy-start | bytes 7077892
  12.2 11.7 %all-to-all-start = ((bf16[4,2,24576]{2,1,0:T(2,128)(2,1)}), bf16[4,2,24576]{2,1,0:T(2,128)(2,1)S(1)}, u32[]{:S(2)}, u32[]{:S(2)}) async-start(bf16[4,2,24576]{2,1,0:T(2,128)(2,1)} %reshape.103), calls=%async_computation | async-start | bytes 786432 | tf_op jit(solution)/shard_map/all_to_all | solution.py:45
  40.1 18.7 %copy-start.12 = (s32[1024]{0:T(1024)S(1)}, s32[1024]{0:T(1024)}, u32[]{:S(2)}) copy-start(s32[1024]{0:T(1024)} %param.17) | copy-start | bytes 12292
  42.0 10.9 %all-to-all-start.1 = ((bf16[16,48,256]{2,0,1:T(8,128)(2,1)}), bf16[16,48,256]{2,0,1:T(8,128)(2,1)S(1)}, u32[]{:S(2)}, u32[]{:S(2)}) async-start(bf16[16,48,256]{2,0,1:T(8,128)(2,1)} %copy.94), calls=%async_computation.1 | async-start | bytes 786432 | tf_op jit(solution)/shard_map/all_to_all | solution.py:49
  53.6 19.5 %collective-permute-start.1 = (bf16[16,12,8,128]{3,0,2,1:T(8,128)(2,1)S(1)}, bf16[16,12,8,128]{3,0,2,1:T(8,128)(2,1)S(1)}, u32[]{:S(2)}, u32[]{:S(2)}) collective-permute-start(bf16[16,12,8,128]{3,0,2,1:T(8,128)(2,1)S(1)} %copy.96), channel_id=1, source_target_pairs={{4,0},{8,4},{12,8},{16,12},{20,16},{24,20},{28,24},{0,28},{5,1},{9... | collective-permute-start | bytes 1179656 | tf_op jit(solution)/shard_map/ppermute | solution.py:18
  58.8 14.5 %collective-permute-start = (bf16[16,12,8,128]{3,0,2,1:T(8,128)(2,1)S(1)}, bf16[16,12,8,128]{3,0,2,1:T(8,128)(2,1)S(1)}, u32[]{:S(2)}, u32[]{:S(2)}) collective-permute-start(bf16[16,12,8,128]{3,0,2,1:T(8,128)(2,1)S(1)} %copy.96), channel_id=1, source_target_pairs={{0,4},{4,8},{8,12},{12,16},{16,20},{20,24},{24,28},{28,0},{1,5},{5... | collective-permute-start | bytes 1179656 | tf_op jit(solution)/shard_map/ppermute | solution.py:16
  76.0 8.8 %copy-start.2 = (bf16[4,12,2,8,256]{4,3,0,2,1:T(8,128)(2,1)S(1)}, bf16[4,12,2,8,256]{4,3,0,2,1:T(8,128)(2,1)}, u32[]{:S(2)}) copy-start(bf16[4,12,2,8,256]{4,3,0,2,1:T(8,128)(2,1)} %copy.126) | copy-start | bytes 1179652
  76.0 8.8 %copy-start.6 = (bf16[16,12,1024]{2,0,1:T(8,128)(2,1)S(1)}, bf16[16,12,1024]{2,0,1:T(8,128)(2,1)}, u32[]{:S(2)}) copy-start(bf16[16,12,1024]{2,0,1:T(8,128)(2,1)} %param.10) | copy-start | bytes 1179652
  76.0 8.8 %copy-start.7 = (f32[12,1024]{1,0:T(8,128)S(1)}, f32[12,1024]{1,0:T(8,128)}, u32[]{:S(2)}) copy-start(f32[12,1024]{1,0:T(8,128)} %compare_convert_fusion) | copy-start | bytes 147460
  76.0 8.8 %copy-start.10 = (f32[12,1024]{1,0:T(8,128)S(1)}, f32[12,1024]{1,0:T(8,128)}, u32[]{:S(2)}) copy-start(f32[12,1024]{1,0:T(8,128)} %param.14) | copy-start | bytes 147460
  85.5 114.5 %copy-start.1 = (bf16[16,12,1024]{2,0,1:T(8,128)(2,1)}, bf16[16,12,1024]{2,0,1:T(8,128)(2,1)S(1)}, u32[]{:S(2)}) copy-start(bf16[16,12,1024]{2,0,1:T(8,128)(2,1)S(1)} %fusion.20) | copy-start | bytes 1179652
  122.5 15.6 %copy-start.9 = (bf16[16,12,1024]{2,0,1:T(8,128)(2,1)S(1)}, bf16[16,12,1024]{2,0,1:T(8,128)(2,1)}, u32[]{:S(2)}) copy-start(bf16[16,12,1024]{2,0,1:T(8,128)(2,1)} %param.16) | copy-start | bytes 1179652
  133.1 54.4 %collective-permute-start.3 = (bf16[16,12,8,128]{3,0,2,1:T(8,128)(2,1)S(1)}, bf16[16,12,8,128]{3,0,2,1:T(8,128)(2,1)S(1)}, u32[]{:S(2)}, u32[]{:S(2)}) collective-permute-start(bf16[16,12,8,128]{3,0,2,1:T(8,128)(2,1)S(1)} %copy.110), channel_id=1, source_target_pairs={{4,0},{8,4},{12,8},{16,12},{20,16},{24,20},{28,24},{0,28},{5,1},{9... | collective-permute-start | bytes 1179656 | tf_op jit(solution)/shard_map/ppermute | solution.py:18
  138.0 49.5 %collective-permute-start.2 = (bf16[16,12,8,128]{3,0,2,1:T(8,128)(2,1)S(1)}, bf16[16,12,8,128]{3,0,2,1:T(8,128)(2,1)}, u32[]{:S(2)}, u32[]{:S(2)}) collective-permute-start(bf16[16,12,8,128]{3,0,2,1:T(8,128)(2,1)S(1)} %copy.110), channel_id=1, source_target_pairs={{0,4},{4,8},{8,12},{12,16},{16,20},{20,24},{24,28},{28,0},{1,5},{5... | collective-permute-start | bytes 1179656 | tf_op jit(solution)/shard_map/ppermute | solution.py:16
  138.1 49.5 %copy-start.3 = (bf16[4,12,2,8,256]{4,3,0,2,1:T(8,128)(2,1)}, bf16[4,12,2,8,256]{4,3,0,2,1:T(8,128)(2,1)S(1)}, u32[]{:S(2)}) copy-start(bf16[4,12,2,8,256]{4,3,0,2,1:T(8,128)(2,1)S(1)} %copy.128) | copy-start | bytes 1179652
  191.3 8.7 %copy-start.4 = (bf16[4,12,2,8,256]{4,3,0,2,1:T(8,128)(2,1)S(1)}, bf16[4,12,2,8,256]{4,3,0,2,1:T(8,128)(2,1)}, u32[]{:S(2)}) copy-start(bf16[4,12,2,8,256]{4,3,0,2,1:T(8,128)(2,1)} %copy-done.3) | copy-start | bytes 1179652
  191.3 8.7 %copy-start.8 = (f32[12,1024]{1,0:T(8,128)S(1)}, f32[12,1024]{1,0:T(8,128)}, u32[]{:S(2)}) copy-start(f32[12,1024]{1,0:T(8,128)} %compare_convert_fusion) | copy-start | bytes 147460
  191.3 8.7 %copy-start.11 = (f32[12,1024]{1,0:T(8,128)S(1)}, f32[12,1024]{1,0:T(8,128)}, u32[]{:S(2)}) copy-start(f32[12,1024]{1,0:T(8,128)} %param.14) | copy-start | bytes 147460
where the time goes:
time: 202 us; the launch traced here: 201 us
  blocking collectives  68.3 us (34%)
  local copies, waits for them, and re-layouts  56.2 us (28%)
  matrix products  29.6 us (15%)
  waiting for transfers between devices  22.4 us (11%)
  starting transfers between devices  17.9 us (9%)
  other arithmetic  6.09 us (3%)
    psum x1, blocking collectives, per_device(): partials.append(lax.psum(local_terms, ('horiz', 'depth')))  48.5 us
    unnamed x34, local copies, waits for them, and re-layouts  31.8 us
    dot_general x2, matrix products, per_device(): jnp.einsum('lrkij,tlrkj->tlri', transport, picked, preferred_element_type...  17.4 us
    ppermute x2, waiting for transfers between devices, padded(): lax.ppermute(head, axis, [((i + 1) % count, i) for i in range(count)])  12.8 us
    all_to_all x6, local copies, waits for them, and re-layouts, per_device(): lax.all_to_all(state, 'depth', split_axis=2, concat_axis=1, tiled=True)  12.3 us
    ppermute x2, starting transfers between devices, padded(): lax.ppermute(head, axis, [((i + 1) % count, i) for i in range(count)])  10.2 us
    dot_general x2, matrix products, per_device(): jnp.einsum('pqc,tpc->tqc', inv_mix, full.astype(jnp.float32), precision=l...  10.1 us
    all_to_all x1, blocking collectives, per_device(): lax.all_to_all(mixed_cols, 'depth', split_axis=1, concat_axis=2, tiled=True)  9.97 us
  transfers between devices with their start and end apart: 6, of which 4 were waited for; matrix products, arithmetic and copies ran while one was open for 4% of the time, Pallas kernels for 0%

commit v1 on v0

v1 whole, which is shorter than its diff:
```python
import functools
import math

import jax
import jax.numpy as jnp
from jax import lax
from jax.experimental import pallas as pl
from jax.experimental.pallas import tpu as pltpu
from jax.sharding import PartitionSpec as P

CHUNKS = 4
LANES = 128
MESH = pl.DeviceIdType.MESH


def flip(index, stride):
    return index + stride * (1 - 2 * ((index // stride) % 2))


def kernel(nh, nd, dims, *refs):
    tr, lev, blocks, slots = dims
    lc = lev // CHUNKS
    pair = blocks // nd
    pad = -(-lev // 8) * 8
    rounds = [("depth", 1 << i) for i in range(nd.bit_length() - 1)]
    rounds += [("horiz", 1 << i) for i in range(nh.bit_length() - 1)]

    (rows_ref, seed_ref, trans_hbm, inv_hbm, rates_ref, coup_ref, sens_ref, count_ref) = refs[:8]
    first_ref, second_ref, grad_ref = refs[8:11]
    rest = list(refs[11:])
    trans, inv, stage_a, stage_b, senst, zacc, gacc, gsend, grecv = rest[:9]
    vs = rest[9:11]
    vfull = rest[11:13]
    zsend = rest[13:15]
    near = [rest[15 : 15 + CHUNKS], rest[15 + CHUNKS : 15 + 2 * CHUNKS]]
    (tsem, isem, vss, vrs, zss, zrs, pss, prs, fss, frs, gss, grs) = rest[15 + 2 * CHUNKS :]

    h = lax.axis_index("horiz")
    d = lax.axis_index("depth")
    odd = h % 2
    partner = h + 1 - 2 * odd
    ahead = (h + 2 - 4 * odd + nh) % nh
    behind = (h - 2 + 4 * odd + nh) % nh
    seen = 2 * blocks * (1 - odd)
    peers = [(d + k) % nd for k in range(nd)]

    inv_copy = pltpu.make_async_copy(inv_hbm, inv, isem)
    inv_copy.start()
    trans_copies = []
    for c in range(CHUNKS):
        part = pl.ds(c * lc, lc)
        trans_copies.append(pltpu.make_async_copy(trans_hbm.at[part], trans.at[part], tsem.at[c]))
        trans_copies[-1].start()

    barrier = pltpu.get_barrier_semaphore()
    greet = [(h, peers[k]) for k in range(1, nd)] + [(ahead, d), (behind, d)]
    greet += [(flip(h, s), d) for axis, s in rounds if axis == "horiz"]
    for device in greet:
        pl.semaphore_signal(barrier, inc=1, device_id=device, device_id_type=MESH)

    def spread(src, stage):
        def one(t, _):
            row = src[t].astype(jnp.float32)
            for b in range(blocks):
                stage[b, pl.ds(pl.multiple_of(t * pad, 8), lev), :] = row[:, b * LANES : (b + 1) * LANES]
            return 0

        lax.fori_loop(0, tr, one, 0)

    def gather(src, out):
        def one(t, _):
            for b in range(blocks):
                row = src[b, pl.ds(pl.multiple_of(t * pad, 8), lev), :]
                out[t, :, cols(b)] = row.astype(jnp.bfloat16)
            return 0

        lax.fori_loop(0, tr, one, 0)

    def cols(b):
        return pl.ds(b * LANES, LANES)

    def keep_own(a, c):
        part = pl.ds(c * lc, lc)
        vfull[a][d, part] = vs[a][d, part]

    sent = []

    def send_v(a, c):
        part = pl.ds(c * lc, lc)
        keep_own(a, c)
        copies = []
        for k in range(1, nd):
            copy = pltpu.make_async_remote_copy(
                src_ref=vs[a].at[peers[k], part],
                dst_ref=vfull[a].at[d, part],
                send_sem=vss.at[a, c, k - 1],
                recv_sem=vrs.at[a, c, k - 1],
                device_id=(h, peers[k]),
                device_id_type=MESH,
            )
            copy.start()
            copies.append(copy)
        sent.extend(copies)
        return copies

    def mix_rows(a, c, blk, rows, accs):
        def body(i, accs):
            s, j = i // lc, c * lc + i % lc
            v = vfull[a][s, j, blk].astype(jnp.float32)
            return tuple(
                acc + inv[s * lev + j, q : q + 1, cols(blk)] * v for acc, q in zip(accs, rows)
            )

        return lax.fori_loop(0, nd * lc, body, tuple(accs), unroll=True)

    def mix_pass(a, c):
        for g in range(nd):
            for blk in range(pair):
                if c == 0:
                    accs = [jnp.zeros((tr, LANES), jnp.float32)] * lev
                else:
                    accs = [zacc[g, l, blk] for l in range(lev)]
                accs = mix_rows(a, c, blk, range(g * lev, (g + 1) * lev), accs)
                for l, acc in enumerate(accs):
                    zacc[g, l, blk] = acc

    def mix_last(a, z):
        spots = [(g, z * lc + j) for g in range(nd) for j in range(lc)]
        for blk in range(pair):
            accs = [zacc[g, l, blk] for g, l in spots]
            accs = mix_rows(a, CHUNKS - 1, blk, [g * lev + l for g, l in spots], accs)
            for i, acc in enumerate(accs):
                zsend[a][i // lc, z, blk, i % lc] = acc.astype(jnp.bfloat16)
        near[a][z][pl.ds(blocks + pair * d, pair)] = zsend[a][d, z]
        copies = []
        for k in range(1, nd):
            copy = pltpu.make_async_remote_copy(
                src_ref=zsend[a].at[peers[k], z],
                dst_ref=near[a][z].at[pl.ds(blocks + pair * d, pair)],
                send_sem=zss.at[a, z, k - 1],
                recv_sem=zrs.at[a, z, k - 1],
                device_id=(h, peers[k]),
                device_id_type=MESH,
            )
            copy.start()
            copies.append(copy)
        sent.extend(copies)
        return copies

    def wet(l, b):
        return count_ref[:, cols(b)] > d * lev + l

    def to_partner(a, z, back):
        for copy in back:
            copy.wait_recv()
        copy = pltpu.make_async_remote_copy(
            src_ref=near[a][z].at[pl.ds(blocks, blocks)],
            dst_ref=near[a][z].at[pl.ds(2 * blocks - seen, blocks)],
            send_sem=pss.at[a, z],
            recv_sem=prs.at[a, z],
            device_id=(partner, d),
            device_id_type=MESH,
        )
        copy.start()
        sent.append(copy)

        def one(j, g):
            for b in range(blocks):
                l = z * lc + j
                value = near[a][z][blocks + b, j].astype(jnp.float32) * senst[l, b]
                g = g + jnp.where(wet(l, b), value, 0.0)
            return g

        gacc[...] = lax.fori_loop(0, lc, one, gacc[...])
        return copy

    def onward(a, z, arrived):
        arrived.wait_recv()
        copy = pltpu.make_async_remote_copy(
            src_ref=near[a][z].at[pl.ds(seen, blocks)],
            dst_ref=near[a][z].at[pl.ds(2 * blocks - seen, blocks)],
            send_sem=fss.at[a, z],
            recv_sem=frs.at[a, z],
            device_id=(ahead, d),
            device_id_type=MESH,
        )
        copy.start()
        sent.append(copy)
        return copy

    def apply(a, z, arrived):
        arrived.wait_recv()
        stage = (stage_a, stage_b)[a]
        if a == 0:
            trans_copies[z].wait()
        where = [[rows_ref[b, k] for k in range(slots)] for b in range(blocks)]
        coup = coup_ref[...]

        def one(j, _):
            l = z * lc + j
            for b in range(blocks):
                own = near[a][z][blocks + b, j]
                picked = [own] + [near[a][z][where[b][k], j] for k in range(1, slots)]
                moved = lax.dot_general(
                    jnp.concatenate(picked, axis=1),
                    jnp.concatenate([trans[l, b, k] for k in range(slots)], axis=1),
                    (((1,), (1,)), ((), ())),
                    preferred_element_type=jnp.float32,
                )
                source = jnp.dot(
                    coup, jnp.concatenate([own, own], axis=0), preferred_element_type=jnp.float32
                )
                source = rates_ref[l, :, cols(b)] * source
                old = vs[a][b // pair, l, b % pair].astype(jnp.float32)
                new = jnp.where(wet(l, b), moved + source - old, 0.0)
                stage[b, pl.ds(l, tr, stride=pad), :] = new
                if a == 0:
                    vs[1][b // pair, l, b % pair] = new.astype(jnp.bfloat16)
            return 0

        lax.fori_loop(0, lc, one, 0)

    spread(seed_ref, stage_a)
    pl.semaphore_wait(barrier, len(greet))
    v_in = [[], []]
    for c in range(CHUNKS):

        def seed_level(j, _):
            l = c * lc + j
            for b in range(blocks):
                tile = stage_a[b, pl.ds(l, tr, stride=pad), :]
                vs[0][b // pair, l, b % pair] = tile.astype(jnp.bfloat16)
            return 0

        lax.fori_loop(0, lc, seed_level, 0)
        v_in[0].append(send_v(0, c))

    spread(sens_ref, stage_b)

    def sens_level(l, _):
        for b in range(blocks):
            senst[l, b] = stage_b[b, pl.ds(l, tr, stride=pad), :]
        return 0

    lax.fori_loop(0, lev, sens_level, 0)
    gacc[...] = jnp.zeros_like(gacc)
    inv_copy.wait()

    def mix_wait(a, c):
        for copy in v_in[a][c]:
            copy.wait_recv()
        if c < CHUNKS - 1:
            mix_pass(a, c)

    gstate = {"round": 0, "copy": None}

    def grad_step():
        r = gstate["round"]
        if gstate["copy"] is not None:
            gstate["copy"].wait_recv()
            gsend[r] = gsend[r - 1] + grecv[r - 1]
            gstate["copy"] = None
        if r < len(rounds):
            axis, s = rounds[r]
            device = (h, flip(d, s)) if axis == "depth" else (flip(h, s), d)
            copy = pltpu.make_async_remote_copy(
                src_ref=gsend.at[r],
                dst_ref=grecv.at[r],
                send_sem=gss.at[r],
                recv_sem=grs.at[r],
                device_id=device,
                device_id_type=MESH,
            )
            copy.start()
            sent.append(copy)
            gstate["copy"] = copy
            gstate["round"] = r + 1

    for c in range(CHUNKS - 1):
        mix_wait(0, c)
    for a in range(2):
        mix_wait(a, CHUNKS - 1)
        back = [mix_last(a, z) for z in range(CHUNKS)]
        if a == 1:
            gather(stage_a, first_ref)
        crossing, forward = [], []

        def finish(z):
            apply(a, z, forward[z])
            if a == 0:
                v_in[1].append(send_v(1, z))
                if z > 0:
                    mix_wait(1, z - 1)

        for z in range(CHUNKS):
            while len(crossing) < min(CHUNKS, z + 2):
                crossing.append(to_partner(a, len(crossing), back[len(crossing)]))
            forward.append(onward(a, z, crossing[z]))
            if z + 2 < CHUNKS:
                crossing.append(to_partner(a, z + 2, back[z + 2]))
            if a == 1 and len(crossing) == CHUNKS:
                if gstate["round"] == 0:
                    gsend[0] = gacc[...]
                grad_step()
            if z > 0:
                finish(z - 1)
        if a == 1:
            grad_step()
        finish(CHUNKS - 1)
    gather(stage_b, second_ref)
    while gstate["copy"] is not None:
        grad_step()
    total = jnp.sum(gsend[len(rounds)], axis=1, keepdims=True)
    scale = math.sqrt(lev * nd * blocks * nh * LANES)
    grad_ref[...] = jnp.broadcast_to(total / scale, (tr, LANES))
    for copy in sent:
        copy.wait_send()


def per_device(nh, nd, seed, transport, neighbours, inv_mix, rates, coupling, sensitivity, count):
    tr, lev, _ = seed.shape
    blocks, slots = neighbours.shape
    lc = lev // CHUNKS
    pair = blocks // nd
    pad = -(-lev // 8) * 8
    n_rounds = nd.bit_length() + nh.bit_length() - 2
    ids = lax.axis_index("horiz") * blocks + jnp.arange(blocks, dtype=jnp.int32)
    steps = (neighbours - ids[:, None] + blocks) % (blocks * nh)
    rows = jnp.arange(blocks, dtype=jnp.int32)[:, None] + steps
    high = coupling.T.astype(jnp.bfloat16)
    low = (coupling.T - high.astype(jnp.float32)).astype(jnp.bfloat16)
    coup = jnp.concatenate([high, low], axis=1)
    bf16, f32 = jnp.bfloat16, jnp.float32
    vmem = pl.BlockSpec(memory_space=pltpu.VMEM)
    hbm = pl.BlockSpec(memory_space=pltpu.HBM)
    tile = (tr, LANES)
    dma = pltpu.SemaphoreType.DMA
    vsem = dma((2, CHUNKS, nd - 1))
    zsem = dma((2, CHUNKS))
    first, second, grad = pl.pallas_call(
        functools.partial(kernel, nh, nd, (tr, lev, blocks, slots)),
        out_shape=(
            jax.ShapeDtypeStruct(seed.shape, bf16),
            jax.ShapeDtypeStruct(seed.shape, bf16),
            jax.ShapeDtypeStruct(tile, f32),
        ),
        in_specs=[
            pl.BlockSpec(memory_space=pltpu.SMEM), vmem, hbm, hbm, vmem, vmem, vmem, vmem,
        ],
        out_specs=(vmem, vmem, vmem),
        scratch_shapes=[
            pltpu.VMEM(transport.shape, bf16),
            pltpu.VMEM(inv_mix.shape, f32),
            pltpu.VMEM((blocks, tr * pad, LANES), f32),
            pltpu.VMEM((blocks, tr * pad, LANES), f32),
            pltpu.VMEM((lev, blocks) + tile, f32),
            pltpu.VMEM((nd, lev, pair) + tile, f32),
            pltpu.VMEM(tile, f32),
            pltpu.VMEM((n_rounds + 1,) + tile, f32),
            pltpu.VMEM((n_rounds,) + tile, f32),
        ]
        + [pltpu.VMEM((nd, lev, pair) + tile, bf16)] * 4
        + [pltpu.VMEM((nd, CHUNKS, pair, lc) + tile, bf16)] * 2
        + [pltpu.VMEM((3 * blocks, lc) + tile, bf16)] * (2 * CHUNKS)
        + [dma((CHUNKS,)), dma]
        + [vsem, vsem, vsem, vsem, zsem, zsem, zsem, zsem, dma((n_rounds,)), dma((n_rounds,))],
        compiler_params=pltpu.CompilerParams(
            collective_id=0, has_side_effects=True, vmem_limit_bytes=44 * 1024 * 1024
        ),
        cost_estimate=pl.CostEstimate(
            flops=4 * transport.size * tr, bytes_accessed=2 * transport.size, transcendentals=0
        ),
    )(rows, seed, transport, inv_mix, rates[:, None, :], coup, sensitivity, count[None, :])
    return first, second, grad[:, 0]


def solution(mesh):
    return jax.shard_map(
        functools.partial(per_device, mesh.shape["horiz"], mesh.shape["depth"]),
        mesh=mesh,
        in_specs=(
            P(None, "depth", "horiz"),
            P("depth", "horiz", None, None, None),
            P("horiz", None),
            P(None, None, ("horiz", "depth")),
            P("depth", "horiz"),
            P(),
            P(None, "depth", "horiz"),
            P("horiz"),
        ),
        out_specs=(P(None, "depth", "horiz"), P(None, "depth", "horiz"), P()),
        check_vma=False,
    )
```

time: 202 us -> 75.5 us (0.37)
  blocking collectives: 68.3 us -> 0 us
  Pallas kernels: 0 us -> 64.6 us
  local copies, waits for them, and re-layouts: 56.2 us -> 8.99 us
  matrix products: 29.6 us -> 0 us
  waiting for transfers between devices: 22.4 us -> 0 us
  starting transfers between devices: 17.9 us -> 0 us
  other arithmetic: 6.09 us -> 0.86 us
    pallas_call x0 -> x1, Pallas kernels: none -> 64.6 us  [per_device(): pl.pallas_call(functools.partial(kernel, nh, nd, (tr, lev, blocks, slots)...]
    psum x1 -> x0, blocking collectives: 48.5 us -> none  [per_device(): partials.append(lax.psum(local_terms, ('horiz', 'depth')))]
    dot_general x6 -> x0, matrix products: 29.6 us -> none  [the longest x2 17.4 us: per_device(): jnp.einsum('lrkij,tlrkj->tlri', transport, picked, preferred_element_type...]
    unnamed x34 -> x9, local copies, waits for them, and re-layouts: 31.8 us -> 7.49 us
    all_to_all x2 -> x0, blocking collectives: 19.8 us -> none  [the longest x1 9.97 us: per_device(): lax.all_to_all(mixed_cols, 'depth', split_axis=1, concat_axis=2, tiled=True)]
    all_to_all x10 -> x0, local copies, waits for them, and re-layouts: 13.7 us -> none  [the longest x6 12.3 us: per_device(): lax.all_to_all(state, 'depth', split_axis=2, concat_axis=1, tiled=True)]
    ppermute x4 -> x0, waiting for transfers between devices: 13 us -> none  [the longest x2 12.8 us: padded(): lax.ppermute(head, axis, [((i + 1) % count, i) for i in range(count)])]
    ppermute x4 -> x0, starting transfers between devices: 10.2 us -> none  [the longest x2 10.2 us: padded(): lax.ppermute(head, axis, [((i + 1) % count, i) for i in range(count)])]
  transfers between devices with their start and end apart: 6 -> 0, of which waited for: 4 -> 0; matrix products, arithmetic and copies ran while one was open for 4% -> 0% of each run, Pallas kernels for 0% -> 0%
where the time goes in v1:
time: 75.5 us; the launch traced here: 75.2 us
  Pallas kernels  64.6 us (86%)
  local copies, waits for them, and re-layouts  8.99 us (12%)
  other arithmetic  0.86 us (1%)
    pallas_call x1, Pallas kernels, per_device(): pl.pallas_call(functools.partial(kernel, nh, nd, (tr, lev, blocks, slots)...  64.6 us
    unnamed x9, local copies, waits for them, and re-layouts  7.49 us

profile of v1, /device:TPU:0, one launch (start us, length us, event | category | flops | bytes accessed | tf_op | source)
XLA Modules:
  0.0 75.2 jit_solution(504733768913611421)
XLA Ops:
  0.6 0.8 %fusion.2.refs_0_ = s32[8,5]{1,0:T(8,128)S(1)} fusion(s32[8,5]{1,0:T(8,128)} %param.10, s32[8]{0:T(128)S(1)} %iota_add_fusion), kind=kLoop, calls=%fused_computation.8 | loop fusion | flops 560 | bytes 352 | tf_op jit(solution)/shard_map/add | solution.py:329
  1.4 0.8 %copy.16 = f32[16,16]{0,1:T(8,128)S(1)} copy(f32[16,16]{1,0:T(8,128)} %param.13) | data formatting | bytes 2048 | tf_op args[5]
  2.2 0.1 pad_maximum_fusion.refs_5_
  2.3 0.9 %broadcast_in_dim.8.refs_4_ = f32[12,1,1024]{2,1,0:T(1,128)S(1)} reshape(f32[12,1024]{1,0:T(8,128)} %param.12) | data formatting | bytes 98304 | tf_op jit(solution)/shard_map/broadcast_in_dim | solution.py:373
  3.1 1.2 %copy.17.refs_1_ = bf16[16,12,1024]{2,1,0:T(8,128)(2,1)S(1)} copy(bf16[16,12,1024]{2,0,1:T(8,128)(2,1)} %param.8) | data formatting | bytes 786432 | tf_op args[0]
  4.4 1.2 %copy.18.refs_6_ = bf16[16,12,1024]{2,1,0:T(8,128)(2,1)S(1)} copy(bf16[16,12,1024]{2,0,1:T(8,128)(2,1)} %param.14) | data formatting | bytes 786432 | tf_op args[6]
  5.6 0.0 copy-start
  5.6 1.7 %copy-done = f32[48,48,256]{2,1,0:T(8,128)S(1)} copy-done((f32[48,48,256]{2,1,0:T(8,128)S(1)}, f32[48,48,256]{2,1,0:T(8,128)}, u32[]{:S(2)}) %copy-start) | copy-done | bytes 2359320
  7.3 0.0 copy-start.1
  7.3 0.7 copy-done.1
  8.0 64.6 %shard_map.103 = (bf16[16,12,1024]{2,1,0:T(8,128)(2,1)S(1)}, bf16[16,12,1024]{2,1,0:T(8,128)(2,1)S(1)}, f32[16,128]{1,0:T(8,128)S(1)}) custom-call(s32[8,5]{1,0:T(8,128)S(1)} %fusion.2.refs_0_, bf16[16,12,1024]{2,1,0:T(8,128)(2,1)S(1)} %copy.17.refs_1_, bf16[12,8,5,128,128]{4,3,2,1,0:T(8,128)(2,1)} %refs_2_.1, f32[48,48,256]{2,1,0:T(8,128)S(1)} %copy-done, ...), custom_call_target="tpu_custom_call" | custom-call | flops 503316480 | bytes 15728640 | tf_op jit(solution)/shard_map/pallas_call | solution.py:340
  72.6 1.0 %copy.19 = bf16[16,12,1024]{2,0,1:T(8,128)(2,1)} copy(bf16[16,12,1024]{2,1,0:T(8,128)(2,1)S(1)} %get-tuple-element.12) | data formatting | bytes 786432
  73.6 0.6 slice_reduce_fusion
  74.2 1.0 %copy.20 = bf16[16,12,1024]{2,0,1:T(8,128)(2,1)} copy(bf16[16,12,1024]{2,1,0:T(8,128)(2,1)S(1)} %get-tuple-element.13) | data formatting | bytes 786432
  (2 shorter events, 0.0 us)
Async XLA Ops:
  5.6 1.7 %copy-start = (f32[48,48,256]{2,1,0:T(8,128)S(1)}, f32[48,48,256]{2,1,0:T(8,128)}, u32[]{:S(2)}) copy-start(f32[48,48,256]{2,1,0:T(8,128)} %refs_3_.1) | copy-start | bytes 7077892
  7.3 0.7 copy-start.1

commit v2 on v1

--- a/solution.py
+++ b/solution.py
@@ -11,6 +11,7 @@
 CHUNKS = 4
 LANES = 128
 MESH = pl.DeviceIdType.MESH
+NT = (((1,), (1,)), ((), ()))
 
 
 def flip(index, stride):
@@ -21,19 +22,19 @@
     tr, lev, blocks, slots = dims
     lc = lev // CHUNKS
     pair = blocks // nd
-    pad = -(-lev // 8) * 8
     rounds = [("depth", 1 << i) for i in range(nd.bit_length() - 1)]
     rounds += [("horiz", 1 << i) for i in range(nh.bit_length() - 1)]
 
-    (rows_ref, seed_ref, trans_hbm, inv_hbm, rates_ref, coup_ref, sens_ref, count_ref) = refs[:8]
+    near_ref, seed_hbm, trans_hbm, inv_hbm, rates_hbm, coup_hbm, sens_hbm, count_hbm = refs[:8]
     first_ref, second_ref, grad_ref = refs[8:11]
     rest = list(refs[11:])
-    trans, inv, stage_a, stage_b, senst, zacc, gacc, gsend, grecv = rest[:9]
-    vs = rest[9:11]
-    vfull = rest[11:13]
-    zsend = rest[13:15]
-    near = [rest[15 : 15 + CHUNKS], rest[15 + CHUNKS : 15 + 2 * CHUNKS]]
-    (tsem, isem, vss, vrs, zss, zrs, pss, prs, fss, frs, gss, grs) = rest[15 + 2 * CHUNKS :]
+    trans, inv, rates, rate_rows, coup_in, coup_ref, sens, count = rest[:8]
+    part_h, zacc, gacc, gsend, grecv = rest[8:13]
+    vs = rest[13:15]
+    vfull = rest[15:17]
+    zsend = rest[17:19]
+    near = [rest[19 : 19 + CHUNKS], rest[19 + CHUNKS : 19 + 2 * CHUNKS]]
+    (ssem, tsem, isem, vss, vrs, zss, zrs, pss, prs, fss, frs, gss, grs) = rest[19 + 2 * CHUNKS :]
 
     h = lax.axis_index("horiz")
     d = lax.axis_index("depth")
@@ -44,40 +45,38 @@
     seen = 2 * blocks * (1 - odd)
     peers = [(d + k) % nd for k in range(nd)]
 
-    inv_copy = pltpu.make_async_copy(inv_hbm, inv, isem)
-    inv_copy.start()
+    def cols(b):
+        return pl.ds(b * LANES, LANES)
+
+    def load(src, dst, sem):
+        copy = pltpu.make_async_copy(src, dst, sem)
+        copy.start()
+        return copy
+
+    seed_copies = [
+        load(seed_hbm.at[:, :, cols(b)], vs[0].at[b // pair, :, b % pair], ssem.at[b])
+        for b in range(blocks)
+    ]
+    inv_copy = load(inv_hbm, inv, isem.at[0])
+    small_copies = [
+        load(src, dst, isem.at[i + 1])
+        for i, (src, dst) in enumerate(
+            [(rates_hbm, rates), (coup_hbm, coup_in), (sens_hbm, sens), (count_hbm, count)]
+        )
+    ]
     trans_copies = []
     for c in range(CHUNKS):
         part = pl.ds(c * lc, lc)
-        trans_copies.append(pltpu.make_async_copy(trans_hbm.at[part], trans.at[part], tsem.at[c]))
-        trans_copies[-1].start()
+        trans_copies.append(load(trans_hbm.at[part], trans.at[part], tsem.at[c]))
+    where = [
+        [near_ref[b, k] for k in range(slots)] for b in range(blocks)
+    ]
 
     barrier = pltpu.get_barrier_semaphore()
     greet = [(h, peers[k]) for k in range(1, nd)] + [(ahead, d), (behind, d)]
     greet += [(flip(h, s), d) for axis, s in rounds if axis == "horiz"]
     for device in greet:
         pl.semaphore_signal(barrier, inc=1, device_id=device, device_id_type=MESH)
-
-    def spread(src, stage):
-        def one(t, _):
-            row = src[t].astype(jnp.float32)
-            for b in range(blocks):
-                stage[b, pl.ds(pl.multiple_of(t * pad, 8), lev), :] = row[:, b * LANES : (b + 1) * LANES]
-            return 0
-
-        lax.fori_loop(0, tr, one, 0)
-
-    def gather(src, out):
-        def one(t, _):
-            for b in range(blocks):
-                row = src[b, pl.ds(pl.multiple_of(t * pad, 8), lev), :]
-                out[t, :, cols(b)] = row.astype(jnp.bfloat16)
-            return 0
-
-        lax.fori_loop(0, tr, one, 0)
-
-    def cols(b):
-        return pl.ds(b * LANES, LANES)
 
     def keep_own(a, c):
         part = pl.ds(c * lc, lc)
@@ -148,7 +147,7 @@
         return copies
 
     def wet(l, b):
-        return count_ref[:, cols(b)] > d * lev + l
+        return count[:, cols(b)] > d * lev + l
 
     def to_partner(a, z, back):
         for copy in back:
@@ -167,7 +166,8 @@
         def one(j, g):
             for b in range(blocks):
                 l = z * lc + j
-                value = near[a][z][blocks + b, j].astype(jnp.float32) * senst[l, b]
+                grade = sens[l, :, cols(b)].astype(jnp.float32)
+                value = near[a][z][blocks + b, j].astype(jnp.float32) * grade
                 g = g + jnp.where(wet(l, b), value, 0.0)
             return g
 
@@ -188,62 +188,72 @@
         sent.append(copy)
         return copy
 
-    def apply(a, z, arrived):
-        arrived.wait_recv()
-        stage = (stage_a, stage_b)[a]
+    def begin(a, z):
         if a == 0:
             trans_copies[z].wait()
-        where = [[rows_ref[b, k] for k in range(slots)] for b in range(blocks)]
         coup = coup_ref[...]
 
         def one(j, _):
             l = z * lc + j
             for b in range(blocks):
                 own = near[a][z][blocks + b, j]
-                picked = [own] + [near[a][z][where[b][k], j] for k in range(1, slots)]
                 moved = lax.dot_general(
-                    jnp.concatenate(picked, axis=1),
-                    jnp.concatenate([trans[l, b, k] for k in range(slots)], axis=1),
-                    (((1,), (1,)), ((), ())),
-                    preferred_element_type=jnp.float32,
+                    own, trans[l, b, 0], NT, preferred_element_type=jnp.float32
                 )
                 source = jnp.dot(
                     coup, jnp.concatenate([own, own], axis=0), preferred_element_type=jnp.float32
                 )
-                source = rates_ref[l, :, cols(b)] * source
+                source = rate_rows[l, :, cols(b)] * source
                 old = vs[a][b // pair, l, b % pair].astype(jnp.float32)
-                new = jnp.where(wet(l, b), moved + source - old, 0.0)
-                stage[b, pl.ds(l, tr, stride=pad), :] = new
+                part_h[l, b] = moved + source - old
+            return 0
+
+        lax.fori_loop(0, lc, one, 0)
+
+    def apply(a, z, arrived):
+        arrived.wait_recv()
+        out = (first_ref, second_ref)[a]
+
+        def one(j, _):
+            l = z * lc + j
+            for b in range(blocks):
+                picked = [near[a][z][where[b][k], j] for k in range(1, slots)]
+                moved = lax.dot_general(
+                    jnp.concatenate(picked, axis=1),
+                    jnp.concatenate([trans[l, b, k] for k in range(1, slots)], axis=1),
+                    NT,
+                    preferred_element_type=jnp.float32,
+                )
+                new = jnp.where(wet(l, b), moved + part_h[l, b], 0.0).astype(jnp.bfloat16)
+                out[l, :, cols(b)] = new
                 if a == 0:
-                    vs[1][b // pair, l, b % pair] = new.astype(jnp.bfloat16)
+                    vs[1][b // pair, l, b % pair] = new
             return 0
 
         lax.fori_loop(0, lc, one, 0)
 
-    spread(seed_ref, stage_a)
+    for copy in seed_copies:
+        copy.wait()
     pl.semaphore_wait(barrier, len(greet))
     v_in = [[], []]
     for c in range(CHUNKS):
-
-        def seed_level(j, _):
-            l = c * lc + j
-            for b in range(blocks):
-                tile = stage_a[b, pl.ds(l, tr, stride=pad), :]
-                vs[0][b // pair, l, b % pair] = tile.astype(jnp.bfloat16)
-            return 0
-
-        lax.fori_loop(0, lc, seed_level, 0)
         v_in[0].append(send_v(0, c))
-
-    spread(sens_ref, stage_b)
-
-    def sens_level(l, _):
-        for b in range(blocks):
-            senst[l, b] = stage_b[b, pl.ds(l, tr, stride=pad), :]
-        return 0
-
-    lax.fori_loop(0, lev, sens_level, 0)
     gacc[...] = jnp.zeros_like(gacc)
+    for copy in small_copies:
+        copy.wait()
+    for l in range(lev):
+        rate_rows[l] = rates[l : l + 1, :]
+    high = coup_in[...].astype(jnp.bfloat16)
+    low = (coup_in[...] - high.astype(jnp.float32)).astype(jnp.bfloat16)
+    unit = lax.broadcasted_iota(jnp.int32, (tr, tr), 0) == lax.broadcasted_iota(
+        jnp.int32, (tr, tr), 1
+    )
+    unit = unit.astype(jnp.float32).astype(jnp.bfloat16)
+    turned = [
+        lax.dot_general(unit, x, NT, preferred_element_type=jnp.float32).astype(jnp.bfloat16)
+        for x in (high, low)
+    ]
+    coup_ref[...] = jnp.concatenate(turned, axis=1)
     inv_copy.wait()
 
     def mix_wait(a, c):
@@ -281,8 +291,6 @@
     for a in range(2):
         mix_wait(a, CHUNKS - 1)
         back = [mix_last(a, z) for z in range(CHUNKS)]
-        if a == 1:
-            gather(stage_a, first_ref)
         crossing, forward = [], []
 
         def finish(z):
@@ -292,27 +300,37 @@
                 if z > 0:
                     mix_wait(1, z - 1)
 
+        def cross():
+            z = len(crossing)
+            if z < CHUNKS:
+                crossing.append(to_partner(a, z, back[z]))
+                begin(a, z)
+                if a == 1 and z == CHUNKS - 1:
+                    gsend[0] = gacc[...]
+                    grad_step()
+
+        cross()
         for z in range(CHUNKS):
-            while len(crossing) < min(CHUNKS, z + 2):
-                crossing.append(to_partner(a, len(crossing), back[len(crossing)]))
+            if z == 0:
+                cross()
+            if a == 1 and z > 1:
+                grad_step()
             forward.append(onward(a, z, crossing[z]))
-            if z + 2 < CHUNKS:
-                crossing.append(to_partner(a, z + 2, back[z + 2]))
-            if a == 1 and len(crossing) == CHUNKS:
-                if gstate["round"] == 0:
-                    gsend[0] = gacc[...]
-                grad_step()
+            cross()
             if z > 0:
                 finish(z - 1)
-        if a == 1:
-            grad_step()
+                if a == 1 and gstate["round"] > 0:
+                    grad_step()
         finish(CHUNKS - 1)
-    gather(stage_b, second_ref)
     while gstate["copy"] is not None:
         grad_step()
-    total = jnp.sum(gsend[len(rounds)], axis=1, keepdims=True)
+    summed = jnp.sum(gsend[len(rounds)], axis=1, keepdims=True)
     scale = math.sqrt(lev * nd * blocks * nh * LANES)
-    grad_ref[...] = jnp.broadcast_to(total / scale, (tr, LANES))
+    summed = jnp.broadcast_to(summed / scale, (tr, LANES))
+    diagonal = lax.broadcasted_iota(jnp.int32, (tr, LANES), 0) == lax.broadcasted_iota(
+        jnp.int32, (tr, LANES), 1
+    )
+    grad_ref[...] = jnp.sum(jnp.where(diagonal, summed, 0.0), axis=0, keepdims=True)
     for copy in sent:
         copy.wait_send()
 
@@ -322,14 +340,11 @@
     blocks, slots = neighbours.shape
     lc = lev // CHUNKS
     pair = blocks // nd
-    pad = -(-lev // 8) * 8
     n_rounds = nd.bit_length() + nh.bit_length() - 2
     ids = lax.axis_index("horiz") * blocks + jnp.arange(blocks, dtype=jnp.int32)
     steps = (neighbours - ids[:, None] + blocks) % (blocks * nh)
     rows = jnp.arange(blocks, dtype=jnp.int32)[:, None] + steps
-    high = coupling.T.astype(jnp.bfloat16)
-    low = (coupling.T - high.astype(jnp.float32)).astype(jnp.bfloat16)
-    coup = jnp.concatenate([high, low], axis=1)
+    seed, sensitivity = (x.transpose(1, 0, 2) for x in (seed, sensitivity))
     bf16, f32 = jnp.bfloat16, jnp.float32
     vmem = pl.BlockSpec(memory_space=pltpu.VMEM)
     hbm = pl.BlockSpec(memory_space=pltpu.HBM)
@@ -342,17 +357,21 @@
         out_shape=(
             jax.ShapeDtypeStruct(seed.shape, bf16),
             jax.ShapeDtypeStruct(seed.shape, bf16),
-            jax.ShapeDtypeStruct(tile, f32),
+            jax.ShapeDtypeStruct((1, LANES), f32),
         ),
         in_specs=[
-            pl.BlockSpec(memory_space=pltpu.SMEM), vmem, hbm, hbm, vmem, vmem, vmem, vmem,
+            pl.BlockSpec(memory_space=pltpu.SMEM), hbm, hbm, hbm, hbm, hbm, hbm, hbm,
         ],
         out_specs=(vmem, vmem, vmem),
         scratch_shapes=[
             pltpu.VMEM(transport.shape, bf16),
             pltpu.VMEM(inv_mix.shape, f32),
-            pltpu.VMEM((blocks, tr * pad, LANES), f32),
-            pltpu.VMEM((blocks, tr * pad, LANES), f32),
+            pltpu.VMEM(rates.shape, f32),
+            pltpu.VMEM((lev, 1, blocks * LANES), f32),
+            pltpu.VMEM(coupling.shape, f32),
+            pltpu.VMEM((tr, 2 * tr), bf16),
+            pltpu.VMEM(sensitivity.shape, bf16),
+            pltpu.VMEM((1, blocks * LANES), jnp.int32),
             pltpu.VMEM((lev, blocks) + tile, f32),
             pltpu.VMEM((nd, lev, pair) + tile, f32),
             pltpu.VMEM(tile, f32),
@@ -362,16 +381,16 @@
         + [pltpu.VMEM((nd, lev, pair) + tile, bf16)] * 4
         + [pltpu.VMEM((nd, CHUNKS, pair, lc) + tile, bf16)] * 2
         + [pltpu.VMEM((3 * blocks, lc) + tile, bf16)] * (2 * CHUNKS)
-        + [dma((CHUNKS,)), dma]
+        + [dma((blocks,)), dma((CHUNKS,)), dma((5,))]
         + [vsem, vsem, vsem, vsem, zsem, zsem, zsem, zsem, dma((n_rounds,)), dma((n_rounds,))],
         compiler_params=pltpu.CompilerParams(
-            collective_id=0, has_side_effects=True, vmem_limit_bytes=44 * 1024 * 1024
+            collective_id=0, has_side_effects=True, vmem_limit_bytes=60 * 1024 * 1024
         ),
         cost_estimate=pl.CostEstimate(
             flops=4 * transport.size * tr, bytes_accessed=2 * transport.size, transcendentals=0
         ),
-    )(rows, seed, transport, inv_mix, rates[:, None, :], coup, sensitivity, count[None, :])
-    return first, second, grad[:, 0]
+    )(rows, seed, transport, inv_mix, rates, coupling, sensitivity, count[None, :])
+    return first.transpose(1, 0, 2), second.transpose(1, 0, 2), grad[0, :tr]
 
 
 def solution(mesh):

time: 75.5 us -> 73.4 us (0.972)
  local copies, waits for them, and re-layouts: 8.99 us -> 4.62 us
  Pallas kernels: 64.6 us -> 66.5 us
    unnamed x9 -> x2, local copies, waits for them, and re-layouts: 7.49 us -> 3.53 us
    pallas_call x1, Pallas kernels: 64.6 us -> 66.5 us  [per_device(): pl.pallas_call(functools.partial(kernel, nh, nd, (tr, lev, blocks, slots)...]
    squeeze x0 -> x1, local copies, waits for them, and re-layouts: none -> 1.09 us  [per_device(): return (first.transpose(1, 0, 2), second.transpose(1, 0, 2), grad[0, :tr])]
    broadcast_in_dim x1 -> x0, local copies, waits for them, and re-layouts: 0.87 us -> none  [per_device(): rates[:, None, :]]
where the time goes in v2:
time: 73.4 us; the launch traced here: 73.2 us
  Pallas kernels  66.5 us (91%)
  local copies, waits for them, and re-layouts  4.62 us (6%)
  other arithmetic  1.36 us (2%)
    pallas_call x1, Pallas kernels, per_device(): pl.pallas_call(functools.partial(kernel, nh, nd, (tr, lev, blocks, slots)...  66.5 us
    unnamed x2, local copies, waits for them, and re-layouts  3.53 us

profile of v2, /device:TPU:0, one launch (start us, length us, event | category | flops | bytes accessed | tf_op | source)
XLA Modules:
  0.0 73.2 jit_solution(1674575358357146468)
XLA Ops:
  0.6 1.4 %fusion.1.refs_0_ = s32[8,5]{1,0:T(8,128)} fusion(s32[8,5]{1,0:T(8,128)} %param.10, s32[8]{0:T(128)S(1)} %iota_add_fusion), kind=kLoop, calls=%fused_computation.4 | loop fusion | flops 560 | bytes 352 | tf_op jit(solution)/shard_map/add | solution.py:346
  2.0 66.5 %shard_map.103 = (bf16[12,16,1024]{2,1,0:T(8,128)(2,1)}, bf16[12,16,1024]{2,1,0:T(8,128)(2,1)}, f32[1,128]{1,0:T(1,128)}) custom-call(s32[8,5]{1,0:T(8,128)} %fusion.1.refs_0_, bf16[12,16,1024]{2,1,0:T(8,128)(2,1)} %bitcast.9, bf16[12,8,5,128,128]{4,3,2,1,0:T(8,128)(2,1)} %refs_2_.1, f32[48,48,256]{2,1,0:T(8,128)} %refs_3_.1, f32[12,1024]{1,0:T(8,128)} %refs_4_.1, ...), custom_call_target="tpu_custom_call" | custom-call | flops 503316480 | bytes 15728640 | tf_op jit(solution)/shard_map/pallas_call | solution.py:355
  68.5 1.1 %slice_bitcast_fusion = f32[16]{0:T(128)} fusion(f32[1,128]{1,0:T(1,128)} %get-tuple-element.8), kind=kLoop, calls=%fused_computation.5 | loop fusion | bytes 128 | tf_op jit(solution)/shard_map/squeeze | solution.py:393
  69.6 1.8 %copy.13 = bf16[16,12,1024]{2,0,1:T(8,128)(2,1)} copy(bf16[16,12,1024]{2,0,1:T(8,128)(2,1)} %bitcast.8) | data formatting | bytes 786432
  71.4 1.8 %copy.14 = bf16[16,12,1024]{2,0,1:T(8,128)(2,1)} copy(bf16[16,12,1024]{2,0,1:T(8,128)(2,1)} %bitcast.7) | data formatting | bytes 786432
  (1 shorter events, 0.0 us)

commit v3 on v2

--- a/solution.py
+++ b/solution.py
@@ -8,7 +8,7 @@
 from jax.experimental.pallas import tpu as pltpu
 from jax.sharding import PartitionSpec as P
 
-CHUNKS = 4
+CHUNKS = 6
 LANES = 128
 MESH = pl.DeviceIdType.MESH
 NT = (((1,), (1,)), ((), ()))
@@ -43,6 +43,7 @@
     ahead = (h + 2 - 4 * odd + nh) % nh
     behind = (h - 2 + 4 * odd + nh) % nh
     seen = 2 * blocks * (1 - odd)
+    total = blocks * nh
     peers = [(d + k) % nd for k in range(nd)]
 
     def cols(b):
@@ -69,7 +70,11 @@
         part = pl.ds(c * lc, lc)
         trans_copies.append(load(trans_hbm.at[part], trans.at[part], tsem.at[c]))
     where = [
-        [near_ref[b, k] for k in range(slots)] for b in range(blocks)
+        [
+            b + jnp.minimum((near_ref[b, k] - (h * blocks + b) + blocks + total) % total, 2 * blocks)
+            for k in range(slots)
+        ]
+        for b in range(blocks)
     ]
 
     barrier = pltpu.get_barrier_semaphore()
@@ -313,7 +318,7 @@
         for z in range(CHUNKS):
             if z == 0:
                 cross()
-            if a == 1 and z > 1:
+            if a == 1 and gstate["round"] > 0:
                 grad_step()
             forward.append(onward(a, z, crossing[z]))
             cross()
@@ -326,13 +331,21 @@
         grad_step()
     summed = jnp.sum(gsend[len(rounds)], axis=1, keepdims=True)
     scale = math.sqrt(lev * nd * blocks * nh * LANES)
-    summed = jnp.broadcast_to(summed / scale, (tr, LANES))
-    diagonal = lax.broadcasted_iota(jnp.int32, (tr, LANES), 0) == lax.broadcasted_iota(
-        jnp.int32, (tr, LANES), 1
+    summed = jnp.broadcast_to(summed / scale, (tr, tr))
+    diagonal = lax.broadcasted_iota(jnp.int32, (tr, tr), 0) == lax.broadcasted_iota(
+        jnp.int32, (tr, tr), 1
     )
     grad_ref[...] = jnp.sum(jnp.where(diagonal, summed, 0.0), axis=0, keepdims=True)
     for copy in sent:
         copy.wait_send()
+
+
+def hand_out(*refs):
+    copies = [pltpu.make_async_copy(refs[i], refs[3 + i], refs[6].at[i]) for i in range(3)]
+    for copy in copies:
+        copy.start()
+    for copy in copies:
+        copy.wait()
 
 
 def per_device(nh, nd, seed, transport, neighbours, inv_mix, rates, coupling, sensitivity, count):
@@ -341,9 +354,6 @@
     lc = lev // CHUNKS
     pair = blocks // nd
     n_rounds = nd.bit_length() + nh.bit_length() - 2
-    ids = lax.axis_index("horiz") * blocks + jnp.arange(blocks, dtype=jnp.int32)
-    steps = (neighbours - ids[:, None] + blocks) % (blocks * nh)
-    rows = jnp.arange(blocks, dtype=jnp.int32)[:, None] + steps
     seed, sensitivity = (x.transpose(1, 0, 2) for x in (seed, sensitivity))
     bf16, f32 = jnp.bfloat16, jnp.float32
     vmem = pl.BlockSpec(memory_space=pltpu.VMEM)
@@ -357,7 +367,7 @@
         out_shape=(
             jax.ShapeDtypeStruct(seed.shape, bf16),
             jax.ShapeDtypeStruct(seed.shape, bf16),
-            jax.ShapeDtypeStruct((1, LANES), f32),
+            jax.ShapeDtypeStruct((1, tr), f32),
         ),
         in_specs=[
             pl.BlockSpec(memory_space=pltpu.SMEM), hbm, hbm, hbm, hbm, hbm, hbm, hbm,
@@ -389,8 +399,17 @@
         cost_estimate=pl.CostEstimate(
             flops=4 * transport.size * tr, bytes_accessed=2 * transport.size, transcendentals=0
         ),
-    )(rows, seed, transport, inv_mix, rates, coupling, sensitivity, count[None, :])
-    return first.transpose(1, 0, 2), second.transpose(1, 0, 2), grad[0, :tr]
+    )(neighbours, seed, transport, inv_mix, rates, coupling, sensitivity, count[None, :])
+    results = (first, second, grad)
+    first, second, grad = pl.pallas_call(
+        hand_out,
+        out_shape=tuple(jax.ShapeDtypeStruct(x.shape, x.dtype) for x in results),
+        in_specs=[hbm] * 3,
+        out_specs=(hbm,) * 3,
+        scratch_shapes=[dma((3,))],
+        compiler_params=pltpu.CompilerParams(vmem_limit_bytes=60 * 1024 * 1024),
+    )(*results)
+    return first.transpose(1, 0, 2), second.transpose(1, 0, 2), grad[0]
 
 
 def solution(mesh):

time: 73.4 us -> 98.4 us (1.34)
  Pallas kernels: 66.5 us -> 97.6 us
  local copies, waits for them, and re-layouts: 4.62 us -> 0 us
  other arithmetic: 1.36 us -> 0 us
    pallas_call x0 -> x1, Pallas kernels: none -> 25 us  [per_device(): pl.pallas_call(hand_out, out_shape=tuple((jax.ShapeDtypeStruct(x.shape, x...]
    pallas_call x1, Pallas kernels: 66.5 us -> 72.6 us  [per_device(): pl.pallas_call(functools.partial(kernel, nh, nd, (tr, lev, blocks, slots)...]
    unnamed x2 -> x0, local copies, waits for them, and re-layouts: 3.53 us -> none
    add x2 -> x0, other arithmetic: 1.36 us -> none  [the longest x1 1.36 us: per_device(): rows = jnp.arange(blocks, dtype=jnp.int32)[:, None] + steps]
    squeeze x1 -> x0, local copies, waits for them, and re-layouts: 1.09 us -> none  [per_device(): return (first.transpose(1, 0, 2), second.transpose(1, 0, 2), grad[0, :tr])]
where the time goes in v3:
time: 98.4 us; the launch traced here: 98.2 us
  Pallas kernels  97.6 us (99%)
    pallas_call x1, Pallas kernels, per_device(): pl.pallas_call(functools.partial(kernel, nh, nd, (tr, lev, blocks, slots)...  72.6 us
    pallas_call x1, Pallas kernels, per_device(): pl.pallas_call(hand_out, out_shape=tuple((jax.ShapeDtypeStruct(x.shape, x...  25 us

profile of v3, /device:TPU:0, one launch (start us, length us, event | category | flops | bytes accessed | tf_op | source)
XLA Modules:
  0.0 98.2 jit_solution(16554895468151436356)
XLA Ops:
  0.6 72.6 %shard_map.103 = (bf16[12,16,1024]{2,1,0:T(8,128)(2,1)}, bf16[12,16,1024]{2,1,0:T(8,128)(2,1)}, f32[1,16]{1,0:T(1,128)}) custom-call(s32[8,5]{1,0:T(8,128)} %refs_0_.1, bf16[12,16,1024]{2,1,0:T(8,128)(2,1)} %bitcast.6, bf16[12,8,5,128,128]{4,3,2,1,0:T(8,128)(2,1)} %refs_2_.1, f32[48,48,256]{2,1,0:T(8,128)} %refs_3_.1, f32[12,1024]{1,0:T(8,128)} %refs_4_.1, ...), custom_call_target="tpu_custom_call" | custom-call | flops 503316480 | bytes 15728640 | tf_op jit(solution)/shard_map/pallas_call | solution.py:365
  73.3 25.0 %shard_map.104 = (bf16[12,16,1024]{2,1,0:T(8,128)(2,1)}, bf16[12,16,1024]{2,1,0:T(8,128)(2,1)}, f32[1,16]{1,0:T(1,128)}) custom-call(bf16[12,16,1024]{2,1,0:T(8,128)(2,1)} %get-tuple-element.9.refs_0_, bf16[12,16,1024]{2,1,0:T(8,128)(2,1)} %get-tuple-element.10.refs_1_, f32[1,16]{1,0:T(1,128)} %get-tuple-element.11.refs_2_), custom_call_target="tpu_custom_call" | custom-call | tf_op jit(solution)/shard_map/pallas_call | solution.py:404

commit v4 on v3

--- a/solution.py
+++ b/solution.py
@@ -8,7 +8,7 @@
 from jax.experimental.pallas import tpu as pltpu
 from jax.sharding import PartitionSpec as P
 
-CHUNKS = 6
+CHUNKS = 3
 LANES = 128
 MESH = pl.DeviceIdType.MESH
 NT = (((1,), (1,)), ((), ()))
@@ -338,14 +338,6 @@
     grad_ref[...] = jnp.sum(jnp.where(diagonal, summed, 0.0), axis=0, keepdims=True)
     for copy in sent:
         copy.wait_send()
-
-
-def hand_out(*refs):
-    copies = [pltpu.make_async_copy(refs[i], refs[3 + i], refs[6].at[i]) for i in range(3)]
-    for copy in copies:
-        copy.start()
-    for copy in copies:
-        copy.wait()
 
 
 def per_device(nh, nd, seed, transport, neighbours, inv_mix, rates, coupling, sensitivity, count):
@@ -400,16 +392,11 @@
             flops=4 * transport.size * tr, bytes_accessed=2 * transport.size, transcendentals=0
         ),
     )(neighbours, seed, transport, inv_mix, rates, coupling, sensitivity, count[None, :])
-    results = (first, second, grad)
-    first, second, grad = pl.pallas_call(
-        hand_out,
-        out_shape=tuple(jax.ShapeDtypeStruct(x.shape, x.dtype) for x in results),
-        in_specs=[hbm] * 3,
-        out_specs=(hbm,) * 3,
-        scratch_shapes=[dma((3,))],
-        compiler_params=pltpu.CompilerParams(vmem_limit_bytes=60 * 1024 * 1024),
-    )(*results)
-    return first.transpose(1, 0, 2), second.transpose(1, 0, 2), grad[0]
+    first, second = (x.transpose(1, 0, 2) for x in (first, second))
+    level_ids = lax.broadcasted_iota(jnp.int32, first.shape, 1) + lax.axis_index("depth") * lev
+    wet = level_ids < count[None, None, :]
+    zero = jnp.zeros((), bf16)
+    return jnp.where(wet, first, zero), jnp.where(wet, second, zero), grad[0]
 
 
 def solution(mesh):

time: 98.4 us -> 68.1 us (0.69)
  Pallas kernels: 97.6 us -> 63.9 us
  other arithmetic: 0 us -> 2.13 us
  local copies, waits for them, and re-layouts: 0 us -> 1.18 us
    pallas_call x1 -> x0, Pallas kernels: 25 us -> none  [per_device(): pl.pallas_call(hand_out, out_shape=tuple((jax.ShapeDtypeStruct(x.shape, x...]
    pallas_call x1, Pallas kernels: 72.6 us -> 63.9 us  [per_device(): pl.pallas_call(functools.partial(kernel, nh, nd, (tr, lev, blocks, slots)...]
    select_n x0 -> x1, other arithmetic: none -> 2.13 us  [per_device(): return (jnp.where(wet, first, zero), jnp.where(wet, second, zero), grad[0])]
    unnamed x0 -> x3, local copies, waits for them, and re-layouts: none -> 1.18 us
where the time goes in v4:
time: 68.1 us; the launch traced here: 67.9 us
  Pallas kernels  63.9 us (94%)
  other arithmetic  2.13 us (3%)
  local copies, waits for them, and re-layouts  1.18 us (2%)
    pallas_call x1, Pallas kernels, per_device(): pl.pallas_call(functools.partial(kernel, nh, nd, (tr, lev, blocks, slots)...  63.9 us
    select_n x1, other arithmetic, per_device(): return (jnp.where(wet, first, zero), jnp.where(wet, second, zero), grad[0])  2.13 us

profile of v4, /device:TPU:0, one launch (start us, length us, event | category | flops | bytes accessed | tf_op | source)
XLA Modules:
  0.0 67.9 jit_solution(2417145389162282486)
XLA Ops:
  0.6 0.0 copy-start
  0.7 63.9 %shard_map.103 = (bf16[12,16,1024]{2,1,0:T(8,128)(2,1)}, bf16[12,16,1024]{2,1,0:T(8,128)(2,1)}, f32[1,16]{1,0:T(1,128)}) custom-call(s32[8,5]{1,0:T(8,128)} %refs_0_.1, bf16[12,16,1024]{2,1,0:T(8,128)(2,1)} %bitcast.8, bf16[12,8,5,128,128]{4,3,2,1,0:T(8,128)(2,1)} %refs_2_.1, f32[48,48,256]{2,1,0:T(8,128)} %refs_3_.1, f32[12,1024]{1,0:T(8,128)} %refs_4_.1, ...), custom_call_target="tpu_custom_call" | custom-call | flops 503316480 | bytes 15728640 | tf_op jit(solution)/shard_map/pallas_call | solution.py:357
  64.6 0.0 copy-done
  64.6 2.1 %compare_select_fusion = (bf16[16,12,1024]{2,0,1:T(8,128)(2,1)}, bf16[16,12,1024]{2,0,1:T(8,128)(2,1)}) fusion(bf16[12,16,1024]{2,1,0:T(8,128)(2,1)} %get-tuple-element.7, s32[1024]{0:T(1024)S(1)} %copy-done, s32[12]{0:T(128)S(1)} %iota_add_fusion, bf16[12,16,1024]{2,1,0:T(8,128)(2,1)} %get-tuple-element.6), kind=kLoop, calls=%fused_computation | loop fusion | flops 589824 | bytes 1577008 | tf_op jit(solution)/shard_map/jit(_where)/select_n | solution.py:399
  66.7 1.2 %copy.12 = f32[16]{0:T(128)} copy(f32[16]{0:T(128)} %bitcast.11) | data formatting | bytes 128
  (1 shorter events, 0.0 us)
Async XLA Ops:
  0.6 63.9 %copy-start = (s32[1024]{0:T(1024)S(1)}, s32[1024]{0:T(1024)}, u32[]{:S(2)}) copy-start(s32[1024]{0:T(1024)} %param.15) | copy-start | bytes 12292
